TPU v7x, 32 devices: a whole 2x2x4 slice. The times are simulated.
32 devices in a mesh: azim: 4 (over y, x), axial: 4 (over z), pair: 2 (over core).
Axes of the slice: x: 2, y: 2, z: 4, core: 2. Of those that a mesh axis runs over, the one named last changes fastest.
Arguments:
- forcing: float32 [64, 160, 256], P('azim', 'axial', 'pair'), may hold values from -12 to 12
- absorption: float32 [64, 160, 256], P('azim', 'axial', 'pair'), may hold values from 0.02 to 2
- blocks: int32 [16, 40, 64], P('azim', 'axial', 'pair'), may hold values 0 or 1
Outputs:
- pressure: float32 [64, 160, 256], P('azim', 'axial', 'pair')
- residual: float32 [64, 160, 256], P('azim', 'axial', 'pair')
All inputs are finite; a program needn't handle non-finite values. No bound on the sum of `blocks` on one device may be relied on, other than what follows from the above.
Results may differ from a plain program's by a relative error of at most 0.0003.
Values sent between devices are 32-bit elements; how exact they have to be, the bound alone decides.
A program may use at most 128 MiB of HBM per device.

v0:
```python
import functools
import jax
import jax.numpy as jnp
from jax import lax
from jax.experimental import pallas as pl
from jax.experimental.pallas import tpu as pltpu
from jax.sharding import PartitionSpec as P

MESH = pl.DeviceIdType.MESH
H = 4
BASE = 12
DAMP = 0.8
KEEP = 0.2
SENDS = 136


def kernel(ng, nz, A, X, f_in, a_in, m_in, p_out, r_out,
           SWF, SWA, SWM, FS, AB, FL, DG, CC, BB, WA, WB, V, V3, RT, TMP,
           SG0, RG0, A1, F1, D1, C1, B1, S1, W1A, W1B, G1S, G1R,
           GL, GA, GB, D2, F2, A2, C2, S2, B2, W2A, W2B, LOC2, T2, AB3, C3, B3, W3A, W3B,
           OST, send_sem, recv_sem):
    az, z, p = lax.axis_index("azim"), lax.axis_index("axial"), lax.axis_index("pair")
    g = az * 2 + p
    own = A // 2
    X1, X2L = X // 2, X // 4
    n2a, x2, n3a, x3 = ng * 2, nz * X2L, ng, nz * X2L // 2
    c3rows = (x3 + 7) // 8 * 8
    lane = lax.broadcasted_iota(jnp.int32, (1, 128), 1)
    counter = [0]

    def dev(gg, zz):
        return (gg // 2, zz, lax.rem(gg, 2))

    def gshift(o):
        return lax.rem(g + o + ng, ng)

    has_lo, has_hi = z > 0, z < nz - 1

    for ref in (FS, AB, FL, WA, WB, V3, A1, F1, W1A, W1B, W2A, W2B, W3A, W3B, C3, B3, AB3, LOC2):
        @pl.loop(0, ref.shape[1])
        def _(a, ref=ref):
            for h in range(2):
                ref[h, a] = jnp.zeros(ref.shape[2:], jnp.float32)
    for c in range(2):
        for h in range(2):
            S1[c, h] = jnp.zeros(S1.shape[2:], jnp.float32)
    bar = pltpu.get_barrier_semaphore()
    for o in range(1, ng):
        pl.semaphore_signal(bar, inc=1, device_id=dev(gshift(o), z), device_id_type=MESH)
    for o in range(1, nz):
        pl.semaphore_signal(bar, inc=1, device_id=dev(g, lax.rem(z + o, nz)), device_id_type=MESH)
    for cond, dz in ((has_lo, -1), (has_hi, 1)):
        @pl.when(cond)
        def _():
            for o in (-1, 1):
                pl.semaphore_signal(bar, inc=1, device_id=dev(gshift(o), z + dz), device_id_type=MESH)
    lows = jnp.where(has_lo, 2, 0) + jnp.where(has_hi, 2, 0)

    pl.semaphore_wait(bar, (ng - 1) + (nz - 1) + lows)

    def remote(src, dst, target, cond=None):
        k = counter[0]
        counter[0] += 1
        def make():
            return pltpu.make_async_remote_copy(
                src_ref=src, dst_ref=dst, send_sem=send_sem.at[k], recv_sem=recv_sem.at[k],
                device_id=target, device_id_type=MESH)
        if cond is None:
            make().start()
        else:
            pl.when(cond)(lambda: make().start())
        return make

    def finish(pairs):
        for make, cs, cr in pairs:
            if cs is None:
                make().wait_send()
                make().wait_recv()
            else:
                pl.when(cs)(lambda make=make: make().wait_send())
                pl.when(cr)(lambda make=make: make().wait_recv())

    def partner(y, s):
        return jnp.where((lane // s) % 2 == 0, pltpu.roll(y, 128 - s, 1), pltpu.roll(y, s, 1))

    def halo_start(buf, stg, rcv, ha, n, r0, nrows, hs=None):
        hs = ha if hs is None else hs
        last = BASE + nrows - H
        @pl.loop(0, n)
        def _(a):
            for h in range(2):
                stg[0, h, a] = buf[h, ha + a, BASE:BASE + H]
                stg[1, h, a] = buf[h, ha + a, last:last + H]
        end = r0
        out = []
        for o in (-1, 1):
            s0 = ha if o < 0 else ha + n - hs
            d0 = ha + n if o < 0 else ha - hs
            out.append((remote(buf.at[:, pl.ds(s0, hs), pl.ds(8, end)],
                               buf.at[:, pl.ds(d0, hs), pl.ds(8, end)],
                               dev(gshift(o), z)), None, None))
        for side, dz, cs, cr in ((0, -1, has_lo, has_hi), (1, 1, has_hi, has_lo)):
            for o in (-1, 0, 1):
                if o == 0:
                    src = stg.at[side]
                    dst = rcv.at[1 - side, :, pl.ds(ha, n)]
                else:
                    s0 = 0 if o < 0 else n - hs
                    d0 = ha + n if o < 0 else ha - hs
                    src = stg.at[side, :, pl.ds(s0, hs)]
                    dst = rcv.at[1 - side, :, pl.ds(d0, hs)]
                out.append((remote(src, dst, dev(gshift(o), z + dz), cs), cs, cr))
        return out

    def halo_place(buf, rcv, ha, n, nrows, hs=None):
        hs = ha if hs is None else hs
        for side, cond, row in ((0, has_lo, BASE - H), (1, has_hi, BASE + nrows)):
            @pl.when(cond)
            def _():
                @pl.loop(ha - hs, n + ha + hs)
                def _(a):
                    for h in range(2):
                        buf[h, a, row:row + H] = rcv[side, h, a]
            @pl.when(jnp.logical_not(cond))
            def _():
                @pl.loop(ha - hs, n + ha + hs)
                def _(a):
                    for h in range(2):
                        buf[h, a, row:row + H] = jnp.zeros((H, 128), jnp.float32)

    def beside(buf, a, up, dn, r0, n, s):
        cen = [buf[h, a, pl.ds(r0, n)] for h in range(2)]
        lf = [pltpu.roll(v, s, 1) for v in cen]
        rt = [pltpu.roll(v, 128 - s, 1) for v in cen]
        left = [jnp.where(lane < s, 0.0, lf[0]), jnp.where(lane < s, lf[0], lf[1])]
        right = [jnp.where(lane >= 128 - s, rt[1], rt[0]), jnp.where(lane >= 128 - s, 0.0, rt[1])]
        tot = []
        for h in range(2):
            t = buf[h, up, pl.ds(r0, n)] + buf[h, dn, pl.ds(r0, n)]
            t = t + buf[h, a, pl.ds(r0 + 1, n)] + buf[h, a, pl.ds(r0 - 1, n)]
            tot.append(t + left[h] + right[h])
        return cen, tot

    def sweep(dst, src, b, c, lo, hi, r0, n, s, ring=None, bidx=None):
        @pl.loop(lo, hi)
        def _(a):
            up, dn = (a + 1, a - 1) if ring is None else (lax.rem(a + 1, ring), lax.rem(a + ring - 1, ring))
            cen, tot = beside(src, a, up, dn, r0, n, s)
            for h in range(2):
                dst[h, a, pl.ds(r0, n)] = (KEEP * cen[h] + b[h, a, pl.ds(r0, n)]
                                           + c[h, a, pl.ds(r0, n)] * tot[h])

    other = 1 - p
    sib = (az, z, other)
    mo = own // 4
    sw = []
    for src, dst, n in ((f_in, SWF, own), (a_in, SWA, own), (m_in, SWM, mo)):
        sw.append((remote(src.at[pl.ds(other * n, n)], dst, sib), None, None))
    PXR = X + 2 * H
    P1R = 32

    for src, dst, n, ha in ((f_in, FS, own, H), (a_in, AB, own, H), (m_in, FL, mo, 1)):
        @pl.loop(0, n)
        def _(a, src=src, dst=dst, n=n, ha=ha):
            dst[p, ha + a, BASE:BASE + X] = src[p * n + a]
    finish(sw)
    for src, dst, n, ha in ((SWF, FS, own, H), (SWA, AB, own, H), (SWM, FL, mo, 1)):
        @pl.loop(0, n)
        def _(a, src=src, dst=dst, n=n, ha=ha):
            dst[other, ha + a, BASE:BASE + X] = src[a]

    flight = []
    stages = {}
    for i, (buf, ha, n) in enumerate(((FS, H, own), (AB, H, own), (FL, 1, mo))):
        flight += halo_start(buf, SG0.at[i, :, :, pl.ds(0, n)],
                             RG0.at[i, :, :, pl.ds(0, n + 2 * ha)], ha, n, PXR, X)

    def rows2(n, r0, op):
        return op(TMP[pl.ds(r0, n, stride=2)], TMP[pl.ds(r0 + 1, n, stride=2)])

    @pl.loop(0, own // 2)
    def _(k):
        for h in range(2):
            TMP[0:PXR] = AB[h, H + 2 * k, 8:8 + PXR] + AB[h, H + 2 * k + 1, 8:8 + PXR]
            t = rows2(X1, BASE - 8, jnp.add)
            A1[h, H + k, BASE:BASE + X1] = 0.25 * (t + partner(t, 1))
            TMP[0:PXR] = FL[h, 1 + k // 2, 8:8 + PXR]
            F1[h, H + k, BASE:BASE + X1] = TMP[pl.ds(BASE - 8, X1, stride=2)]
    for i, buf in enumerate((A1, F1)):
        flight += halo_start(buf, G1S.at[i], G1R.at[i], H, own // 2, P1R, X1)

    def restrict2(buf, h, k, op):
        TMP[0:P1R] = op(buf[h, 2 * k, 8:8 + P1R], buf[h, 2 * k + 1, 8:8 + P1R])
        t = rows2(X2L, BASE - 8, op)
        return op(t, partner(t, 2))

    def put(slot, vals):
        y = jnp.where(lane % 4 == 0, vals[0], jnp.where(lane % 4 == 1, vals[1], jnp.where(lane % 4 == 2, vals[2], vals[3])))
        GL[slot, 0:X2L] = y

    def gather(slot, count):
        rs = []
        @pl.loop(0, count)
        def _(i):
            GA[slot + i, z] = GL[slot + i]
        for o in range(1, nz):
            rs.append((remote(GL.at[pl.ds(slot, count)], GA.at[pl.ds(slot, count), z],
                              dev(g, lax.rem(z + o, nz))), None, None))
        finish(rs)
        rs = []
        for o in range(1, ng):
            rs.append((remote(GA.at[pl.ds(slot, count)], GB.at[pl.ds(slot, count), g],
                              dev(gshift(o), z)), None, None))
        for i in range(count):
            for zz in range(nz):
                GB[slot + i, g, zz] = GA[slot + i, zz]
        finish(rs)

    def unpack(slot, dst):
        @pl.loop(0, ng)
        def _(gg):
            for zz in range(nz):
                t = GB[slot, gg, zz]
                for q in range(4):
                    y = jnp.where(lane % 4 == q, t, 0.0)
                    y = y + partner(y, 1)
                    y = y + partner(y, 2)
                    dst[q // 2, 2 * gg + q % 2, pl.ds(8 + X2L * zz, X2L)] = y[0:X2L]

    vals = [0.25 * restrict2(A1.at[:, pl.ds(H, own // 2)], q // 2, q % 2, jnp.add) for q in range(4)]
    put(0, vals)
    vals = [restrict2(F1.at[:, pl.ds(H, own // 2)], q // 2, q % 2, jnp.maximum) for q in range(4)]
    put(1, vals)
    gather(0, 2)
    unpack(0, A2)
    unpack(1, F2)

    R2 = x2
    @pl.loop(0, n2a)
    def _(a):
        for h in range(2):
            f = F2[h, a, pl.ds(8, R2)]
            d = f * (6.0 + A2[h, a, pl.ds(8, R2)]) + 1.0 - f
            D2[h, a, pl.ds(8, R2)] = d
            C2[h, a, pl.ds(8, R2)] = DAMP * f / d

    @pl.loop(0, n3a)
    def _(k):
        for h in range(2):
            T2[0:R2] = A2[h, 2 * k, pl.ds(8, R2)] + A2[h, 2 * k + 1, pl.ds(8, R2)]
            t = T2[pl.ds(0, x3, stride=2)] + T2[pl.ds(1, x3, stride=2)]
            ab = 0.25 * (t + partner(t, 4))
            T2[0:R2] = jnp.maximum(F2[h, 2 * k, pl.ds(8, R2)], F2[h, 2 * k + 1, pl.ds(8, R2)])
            t = jnp.maximum(T2[pl.ds(0, x3, stride=2)], T2[pl.ds(1, x3, stride=2)])
            f = jnp.maximum(t, partner(t, 4))
            C3[h, k, 8:8 + x3] = DAMP * f / (f * (6.0 + ab) + 1.0 - f)

    finish(flight)
    for i, (buf, ha, n) in enumerate(((FS, H, own), (AB, H, own), (FL, 1, mo))):
        halo_place(buf, RG0.at[i, :, :, pl.ds(0, n + 2 * ha)], ha, n, X)
    for i, buf in enumerate((A1, F1)):
        halo_place(buf, G1R.at[i], H, own // 2, X1)

    @pl.loop(0, own + 2 * H)
    def _(a):
        for h in range(2):
            f = FL[h, a // 4, 8:8 + PXR]
            d = f * (6.0 + AB[h, a, 8:8 + PXR]) + 1.0 - f
            c = DAMP * f / d
            DG[h, a, 8:8 + PXR] = d
            CC[h, a, 8:8 + PXR] = c
            BB[h, a, 8:8 + PXR] = c * FS[h, a, 8:8 + PXR]

    @pl.loop(0, own // 2 + 2 * H)
    def _(a):
        for h in range(2):
            f = F1[h, a, 8:8 + P1R]
            d = f * (6.0 + A1[h, a, 8:8 + P1R]) + 1.0 - f
            D1[h, a, 8:8 + P1R] = d
            C1[h, a, 8:8 + P1R] = DAMP * f / d

    def remainder0(buf, a, solid):
        cen, tot = beside(buf, a, a + 1, a - 1, 8, PXR, 1)
        out = []
        for h in range(2):
            f = FL[h, a // 4, 8:8 + PXR]
            s = FS[h, a, 8:8 + PXR]
            out.append(jnp.where(f > 0, s - (DG[h, a, 8:8 + PXR] * cen[h] - tot[h]), solid * s))
        return out

    def level3():
        @pl.loop(0, n3a)
        def _(a):
            for h in range(2):
                W3A[h, a, pl.ds(8, c3rows)] = B3[h, a, pl.ds(8, c3rows)]
        for src, dst in ((W3A, W3B), (W3B, W3A), (W3A, W3B)):
            sweep(dst, src, B3, C3, 0, n3a, 8, c3rows, 8, ring=n3a)
        return W3B

    def level2():
        @pl.loop(0, n2a)
        def _(a):
            for h in range(2):
                b = C2[h, a, pl.ds(8, R2)] * S2[h, a, pl.ds(8, R2)]
                B2[h, a, pl.ds(8, R2)] = b
                W2A[h, a, pl.ds(8, R2)] = b
        sweep(W2B, W2A, B2, C2, 0, n2a, 8, R2, 4, ring=n2a)

        @pl.loop(0, n3a)
        def _(k):
            rem = [0.0, 0.0]
            for j in range(2):
                a = 2 * k + j
                cen, tot = beside(W2B, a, lax.rem(a + 1, n2a), lax.rem(a + n2a - 1, n2a), 8, R2, 4)
                for h in range(2):
                    s = S2[h, a, pl.ds(8, R2)]
                    rem[h] = rem[h] + jnp.where(F2[h, a, pl.ds(8, R2)] > 0,
                                                s - (D2[h, a, pl.ds(8, R2)] * cen[h] - tot[h]), (KEEP * KEEP) * s)
            for h in range(2):
                T2[0:R2] = rem[h]
                t = T2[pl.ds(0, x3, stride=2)] + T2[pl.ds(1, x3, stride=2)]
                B3[h, k, 8:8 + x3] = C3[h, k, 8:8 + x3] * (0.25 * (t + partner(t, 4)))
        w3 = level3()

        @pl.loop(0, n3a)
        def _(k):
            for h in range(2):
                v = w3[h, k, 8:8 + x3]
                T2[pl.ds(0, x3, stride=2)] = v
                T2[pl.ds(1, x3, stride=2)] = v
                t = T2[0:R2]
                for j in range(2):
                    W2A[h, 2 * k + j, pl.ds(8, R2)] = W2B[h, 2 * k + j, pl.ds(8, R2)] + F2[h, 2 * k + j, pl.ds(8, R2)] * t
        sweep(W2B, W2A, B2, C2, 0, n2a, 8, R2, 4, ring=n2a)
        sweep(W2A, W2B, B2, C2, 0, n2a, 8, R2, 4, ring=n2a)
        return W2A

    def level1(cyc):
        src = S1.at[cyc]
        fl = halo_start(src, G1S.at[2 + cyc], G1R.at[2 + cyc], H, own // 2, P1R, X1)
        finish(fl)
        halo_place(src, G1R.at[2 + cyc], H, own // 2, X1)
        n1 = own // 2 + 2 * H

        @pl.loop(0, n1)
        def _(a):
            for h in range(2):
                b = C1[h, a, 8:8 + P1R] * src[h, a, 8:8 + P1R]
                B1[h, a, 8:8 + P1R] = b
                W1A[h, a, 8:8 + P1R] = b
        sweep(W1B, W1A, B1, C1, 1, n1 - 1, 8, P1R, 2)

        vals = {}
        for k in range(2):
            rem = [0.0, 0.0]
            for j in range(2):
                a = H + 2 * k + j
                cen, tot = beside(W1B, a, a + 1, a - 1, 8, P1R, 2)
                for h in range(2):
                    s = src[h, a, 8:8 + P1R]
                    rem[h] = rem[h] + jnp.where(F1[h, a, 8:8 + P1R] > 0,
                                                s - (D1[h, a, 8:8 + P1R] * cen[h] - tot[h]), (KEEP * KEEP) * s)
            for h in range(2):
                TMP[0:P1R] = rem[h]
                t = rows2(X2L, BASE - 8, jnp.add)
                vals[(h, k)] = 0.25 * (t + partner(t, 2))
        put(2 + cyc, [vals[(q // 2, q % 2)] for q in range(4)])
        gather(2 + cyc, 1)
        unpack(2 + cyc, S2)
        w2 = level2()
        nl = own // 4 + 4
        for zz in range(nz):
            @pl.when(z == zz)
            def _(zz=zz):
                @pl.loop(0, nl)
                def _(j):
                    a = lax.rem(own // 4 * g + j - 2 + n2a, n2a)
                    for h in range(2):
                        LOC2[h, j, 0:16] = w2[h, a, 8 + X2L * zz - 2:8 + X2L * zz + 14]

        @pl.loop(0, nl)
        def _(j):
            for h in range(2):
                v = LOC2[h, j, 0:16]
                TMP[pl.ds(0, 16, stride=2)] = v
                TMP[pl.ds(1, 16, stride=2)] = v
                t = TMP[0:P1R]
                for i in range(2):
                    a = 2 * j + i
                    W1A[h, a, 8:8 + P1R] = W1B[h, a, 8:8 + P1R] + F1[h, a, 8:8 + P1R] * t
        sweep(W1B, W1A, B1, C1, 2, n1 - 2, 8, P1R, 2)
        sweep(W1A, W1B, B1, C1, 3, n1 - 3, 8, P1R, 2)
        return W1A

    n0 = own + 2 * H
    for cyc in range(2):
        if cyc == 0:
            sweep(WB, BB, BB, CC, 2, n0 - 2, 8, PXR, 1)
        else:
            fl = halo_start(V, SG0.at[3], RG0.at[3], H, own, PXR, X)
            finish(fl)
            halo_place(V, RG0.at[3], H, own, X)
            sweep(WA, V, BB, CC, 1, n0 - 1, 8, PXR, 1)
            sweep(WB, WA, BB, CC, 2, n0 - 2, 8, PXR, 1)
        solid = KEEP ** (2 if cyc == 0 else 6)

        @pl.loop(0, own // 2)
        def _(k):
            ra = remainder0(WB, H + 2 * k, solid)
            rb = remainder0(WB, H + 2 * k + 1, solid)
            for h in range(2):
                TMP[0:PXR] = ra[h] + rb[h]
                t = rows2(X1, BASE - 8, jnp.add)
                S1[cyc, h, H + k, BASE:BASE + X1] = 0.25 * (t + partner(t, 1))
        w1 = level1(cyc)

        @pl.loop(3, own // 2 + 2 * H - 3)
        def _(k):
            for h in range(2):
                v = w1[h, k, BASE - 2:BASE - 2 + X1 + 4]
                TMP[pl.ds(0, X1 + 4, stride=2)] = v
                TMP[pl.ds(1, X1 + 4, stride=2)] = v
                t = TMP[0:PXR]
                for i in range(2):
                    a = 2 * (k - 2) + i
                    WA[h, a, 8:8 + PXR] = WB[h, a, 8:8 + PXR] + jnp.where(FL[h, a // 4, 8:8 + PXR] > 0, t, 0.0)
        sweep(WB, WA, BB, CC, 3, n0 - 3, 8, PXR, 1)
        sweep(V if cyc == 0 else V3, WB, BB, CC, 4, n0 - 4, 8, PXR, 1)

    fl = halo_start(V3, SG0.at[4], RG0.at[4], H, own, PXR, X, hs=1)
    grown = 1.0 - KEEP ** 8

    @pl.loop(0, own)
    def _(a):
        for h in range(2):
            f = FL[h, 1 + a // 4, BASE:BASE + X]
            OST[0, h, a] = jnp.where(f > 0, V3[h, H + a, BASE:BASE + X], grown * FS[h, H + a, BASE:BASE + X])
    outs = [(remote(OST.at[0, other], p_out.at[pl.ds(p * own, own)], sib), None, None)]
    finish(fl)
    halo_place(V3, RG0.at[4], H, own, X, hs=1)

    @pl.loop(0, own)
    def _(a):
        r = remainder0(V3, H + a, KEEP ** 8)
        for h in range(2):
            OST[1, h, a] = r[h][H:H + X]
    outs.append((remote(OST.at[1, other], r_out.at[pl.ds(p * own, own)], sib), None, None))

    @pl.loop(0, own)
    def _(a):
        p_out[p * own + a] = OST[0, p, a]
        r_out[p * own + a] = OST[1, p, a]
    finish(outs)


def solution(mesh):
    ng = mesh.shape["azim"] * mesh.shape["pair"]
    nz = mesh.shape["axial"]

    def per_device(forcing, absorption, blocks):
        A, X, R = forcing.shape
        own = A // 2
        fl = jnp.repeat(jnp.repeat(blocks.astype(jnp.float32), 4, axis=1), 4, axis=2)
        px, p1 = X + 24, 48
        n0, n1 = own + 2 * H, own // 2 + 2 * H
        x2 = nz * (X // 4)
        n2, r2 = ng * 2, x2 + 16
        n3, r3 = ng, (x2 // 2 + 7) // 8 * 8 + 16
        V = lambda *s: pltpu.VMEM(s, jnp.float32)
        full = V(2, n0, px, 128)
        lev1 = V(2, n1, p1, 128)
        lev2 = V(2, n2, r2, 128)
        lev3 = V(2, n3, r3, 128)
        scratch = [
            V(own, X, 128), V(own, X, 128), V(own // 4, X, 128),
            full, full, V(2, own // 4 + 2, px, 128),
            full, full, full, full, full, full, full, V(8, 128), V(64, 128),
            V(5, 2, 2, own, H, 128), V(5, 2, 2, n0, H, 128),
            lev1, lev1, lev1, lev1, lev1, V(2, 2, n1, p1, 128), lev1, lev1,
            V(4, 2, 2, own // 2, H, 128), V(4, 2, 2, n1, H, 128),
            V(4, 16, 128), V(4, nz, 16, 128), V(4, ng, nz, 16, 128),
            lev2, lev2, lev2, lev2, lev2, lev2, lev2, lev2,
            V(2, own // 4 + 4, 16, 128), V(x2, 128), V(2, 1, 8, 128), lev3, lev3, lev3, lev3,
            V(2, 2, own, X, 128),
            pltpu.SemaphoreType.DMA((SENDS,)), pltpu.SemaphoreType.DMA((SENDS,)),
        ]
        vm = pl.BlockSpec(memory_space=pltpu.VMEM)
        return pl.pallas_call(
            functools.partial(kernel, ng, nz, A, X),
            out_shape=[jax.ShapeDtypeStruct((A, X, R), jnp.float32)] * 2,
            in_specs=[vm] * 3, out_specs=[vm] * 2, scratch_shapes=scratch,
            compiler_params=pltpu.CompilerParams(
                collective_id=0, has_side_effects=True, vmem_limit_bytes=56 * 1024 * 1024),
        )(forcing, absorption, fl)

    spec = P("azim", "axial", "pair")
    return jax.shard_map(per_device, mesh=mesh, in_specs=(spec,) * 3, out_specs=(spec,) * 2, check_vma=False)
```

profile of v0, /device:TPU:0, one launch (start us, length us, event | category | flops | bytes accessed | tf_op | source)
XLA Modules:
  0.0 124.5 jit_solution(13043083647099159635)
XLA Ops:
  0.6 0.7 convert_element_type.3
  1.4 0.1 copy.9
  1.5 0.1 broadcast_in_dim.7
  1.5 0.7 copy.10.m_in
  2.3 119.8 %shard_map.50 = (f32[16,40,128]{2,1,0:T(8,128)}, f32[16,40,128]{2,1,0:T(8,128)}) custom-call(f32[16,40,128]{2,1,0:T(8,128)} %f_in.1, f32[16,40,128]{2,1,0:T(8,128)} %a_in.1, f32[4,40,128]{2,1,0:T(8,128)} %copy.10.m_in), custom_call_target="tpu_custom_call" | custom-call | tf_op jit(solution)/shard_map/pallas_call | solution.py:488
  122.0 0.0 copy-start
  122.1 1.8 %copy.13 = f32[16,40,128]{2,1,0:T(8,128)} copy(f32[16,40,128]{2,1,0:T(8,128)} %get-tuple-element.4) | data formatting | bytes 655360
  123.8 0.0 copy-done
  123.8 0.7 copy.14
  (2 shorter events, 0.0 us)
Async XLA Ops:
  122.0 1.8 %copy-start = (f32[16,40,128]{2,1,0:T(8,128)S(1)}, f32[16,40,128]{2,1,0:T(8,128)}, u32[]{:S(2)}) copy-start(f32[16,40,128]{2,1,0:T(8,128)} %get-tuple-element.5) | copy-start | bytes 983044
where the time goes:
time: 125 us
  Pallas kernels  120 us (96%)
  local copies, waits for them, and re-layouts  3.39 us (3%)
    pallas_call x1, Pallas kernels, per_device(): pl.pallas_call(functools.partial(kernel, ng, nz, A, X), out_shape=[jax.Sh...  120 us

commit v1 on v0

--- a/solution.py
+++ b/solution.py
@@ -17,7 +17,7 @@
 def kernel(ng, nz, A, X, f_in, a_in, m_in, p_out, r_out,
            SWF, SWA, SWM, FS, AB, FL, DG, CC, BB, WA, WB, V, V3, RT, TMP,
            SG0, RG0, A1, F1, D1, C1, B1, S1, W1A, W1B, G1S, G1R,
-           GL, GA, GB, D2, F2, A2, C2, S2, B2, W2A, W2B, LOC2, T2, AB3, C3, B3, W3A, W3B,
+           GL, GA, GB, D2, F2, A2, C2, S2, B2, W2A, W2B, LOC2, T2, AF, C3, B3, W3A, W3B,
            OST, send_sem, recv_sem):
     az, z, p = lax.axis_index("azim"), lax.axis_index("axial"), lax.axis_index("pair")
     g = az * 2 + p
@@ -36,7 +36,7 @@
 
     has_lo, has_hi = z > 0, z < nz - 1
 
-    for ref in (FS, AB, FL, WA, WB, V3, A1, F1, W1A, W1B, W2A, W2B, W3A, W3B, C3, B3, AB3, LOC2):
+    for ref in (WA, WB, AF, W1A, W1B, W2A, W2B, W3A, W3B, C3, B3):
         @pl.loop(0, ref.shape[1])
         def _(a, ref=ref):
             for h in range(2):
@@ -142,7 +142,7 @@
         return cen, tot
 
     def sweep(dst, src, b, c, lo, hi, r0, n, s, ring=None, bidx=None):
-        @pl.loop(lo, hi)
+        @pl.loop(lo, hi, unroll=4)
         def _(a):
             up, dn = (a + 1, a - 1) if ring is None else (lax.rem(a + 1, ring), lax.rem(a + ring - 1, ring))
             cen, tot = beside(src, a, up, dn, r0, n, s)
@@ -173,7 +173,7 @@
     stages = {}
     for i, (buf, ha, n) in enumerate(((FS, H, own), (AB, H, own), (FL, 1, mo))):
         flight += halo_start(buf, SG0.at[i, :, :, pl.ds(0, n)],
-                             RG0.at[i, :, :, pl.ds(0, n + 2 * ha)], ha, n, PXR, X)
+                             RG0.at[i, :, :, pl.ds(0, n + 2 * ha)], ha, n, PXR, X, hs=min(ha, H - 1))
 
     def rows2(n, r0, op):
         return op(TMP[pl.ds(r0, n, stride=2)], TMP[pl.ds(r0 + 1, n, stride=2)])
@@ -183,11 +183,13 @@
         for h in range(2):
             TMP[0:PXR] = AB[h, H + 2 * k, 8:8 + PXR] + AB[h, H + 2 * k + 1, 8:8 + PXR]
             t = rows2(X1, BASE - 8, jnp.add)
-            A1[h, H + k, BASE:BASE + X1] = 0.25 * (t + partner(t, 1))
+            ab = 0.25 * (t + partner(t, 1))
+            A1[h, H + k, BASE:BASE + X1] = ab
             TMP[0:PXR] = FL[h, 1 + k // 2, 8:8 + PXR]
-            F1[h, H + k, BASE:BASE + X1] = TMP[pl.ds(BASE - 8, X1, stride=2)]
-    for i, buf in enumerate((A1, F1)):
-        flight += halo_start(buf, G1S.at[i], G1R.at[i], H, own // 2, P1R, X1)
+            f = TMP[pl.ds(BASE - 8, X1, stride=2)]
+            F1[h, H + k, BASE:BASE + X1] = f
+            AF[h, H + k, BASE:BASE + X1] = jnp.where(lane % 2 == 0, ab, f)
+    flight += halo_start(AF, G1S.at[0], G1R.at[0], H, own // 2, P1R, X1)
 
     def restrict2(buf, h, k, op):
         TMP[0:P1R] = op(buf[h, 2 * k, 8:8 + P1R], buf[h, 2 * k + 1, 8:8 + P1R])
@@ -257,9 +259,8 @@
 
     finish(flight)
     for i, (buf, ha, n) in enumerate(((FS, H, own), (AB, H, own), (FL, 1, mo))):
-        halo_place(buf, RG0.at[i, :, :, pl.ds(0, n + 2 * ha)], ha, n, X)
-    for i, buf in enumerate((A1, F1)):
-        halo_place(buf, G1R.at[i], H, own // 2, X1)
+        halo_place(buf, RG0.at[i, :, :, pl.ds(0, n + 2 * ha)], ha, n, X, hs=min(ha, H - 1))
+    halo_place(AF, G1R.at[0], H, own // 2, X1)
 
     @pl.loop(0, own + 2 * H)
     def _(a):
@@ -274,8 +275,11 @@
     @pl.loop(0, own // 2 + 2 * H)
     def _(a):
         for h in range(2):
-            f = F1[h, a, 8:8 + P1R]
-            d = f * (6.0 + A1[h, a, 8:8 + P1R]) + 1.0 - f
+            t = AF[h, a, 8:8 + P1R]
+            swapped = partner(t, 1)
+            f = jnp.where(lane % 2 == 0, swapped, t)
+            F1[h, a, 8:8 + P1R] = f
+            d = f * (6.0 + jnp.where(lane % 2 == 0, t, swapped)) + 1.0 - f
             D1[h, a, 8:8 + P1R] = d
             C1[h, a, 8:8 + P1R] = DAMP * f / d
 
@@ -480,7 +484,7 @@
             V(4, 2, 2, own // 2, H, 128), V(4, 2, 2, n1, H, 128),
             V(4, 16, 128), V(4, nz, 16, 128), V(4, ng, nz, 16, 128),
             lev2, lev2, lev2, lev2, lev2, lev2, lev2, lev2,
-            V(2, own // 4 + 4, 16, 128), V(x2, 128), V(2, 1, 8, 128), lev3, lev3, lev3, lev3,
+            V(2, own // 4 + 4, 16, 128), V(x2, 128), lev1, lev3, lev3, lev3, lev3,
             V(2, 2, own, X, 128),
             pltpu.SemaphoreType.DMA((SENDS,)), pltpu.SemaphoreType.DMA((SENDS,)),
         ]

time: 125 us -> 106 us (0.85)
  Pallas kernels: 120 us -> 101 us
    pallas_call x1, Pallas kernels: 120 us -> 101 us  [per_device(): pl.pallas_call(functools.partial(kernel, ng, nz, A, X), out_shape=[jax.Sh...]
where the time goes in v1:
time: 106 us
  Pallas kernels  101 us (95%)
  local copies, waits for them, and re-layouts  3.39 us (3%)
    pallas_call x1, Pallas kernels, per_device(): pl.pallas_call(functools.partial(kernel, ng, nz, A, X), out_shape=[jax.Sh...  101 us
    unnamed x4, local copies, waits for them, and re-layouts  2.49 us

profile of v1, /device:TPU:0, one launch (start us, length us, event | category | flops | bytes accessed | tf_op | source)
XLA Modules:
  0.0 105.6 jit_solution(13016606275298876375)
XLA Ops:
  0.6 0.7 convert_element_type.3
  1.4 0.1 copy.9
  1.5 0.1 broadcast_in_dim.7
  1.5 0.7 copy.10.m_in
  2.3 100.8 %shard_map.50 = (f32[16,40,128]{2,1,0:T(8,128)}, f32[16,40,128]{2,1,0:T(8,128)}) custom-call(f32[16,40,128]{2,1,0:T(8,128)} %f_in.1, f32[16,40,128]{2,1,0:T(8,128)} %a_in.1, f32[4,40,128]{2,1,0:T(8,128)} %copy.10.m_in), custom_call_target="tpu_custom_call" | custom-call | tf_op jit(solution)/shard_map/pallas_call | solution.py:492
  103.1 0.0 copy-start
  103.1 1.8 %copy.13 = f32[16,40,128]{2,1,0:T(8,128)} copy(f32[16,40,128]{2,1,0:T(8,128)} %get-tuple-element.4) | data formatting | bytes 655360
  104.9 0.0 copy-done
  104.9 0.7 copy.14
  (2 shorter events, 0.0 us)
Async XLA Ops:
  103.1 1.8 %copy-start = (f32[16,40,128]{2,1,0:T(8,128)S(1)}, f32[16,40,128]{2,1,0:T(8,128)}, u32[]{:S(2)}) copy-start(f32[16,40,128]{2,1,0:T(8,128)} %get-tuple-element.5) | copy-start | bytes 983044

commit v2 on v1

--- a/solution.py
+++ b/solution.py
@@ -142,7 +142,7 @@
         return cen, tot
 
     def sweep(dst, src, b, c, lo, hi, r0, n, s, ring=None, bidx=None):
-        @pl.loop(lo, hi, unroll=4)
+        @pl.loop(lo, hi, unroll=4 if n > 40 else 8)
         def _(a):
             up, dn = (a + 1, a - 1) if ring is None else (lax.rem(a + 1, ring), lax.rem(a + ring - 1, ring))
             cen, tot = beside(src, a, up, dn, r0, n, s)
@@ -302,7 +302,7 @@
         return W3B
 
     def level2():
-        @pl.loop(0, n2a)
+        @pl.loop(0, n2a, unroll=4)
         def _(a):
             for h in range(2):
                 b = C2[h, a, pl.ds(8, R2)] * S2[h, a, pl.ds(8, R2)]
@@ -310,7 +310,7 @@
                 W2A[h, a, pl.ds(8, R2)] = b
         sweep(W2B, W2A, B2, C2, 0, n2a, 8, R2, 4, ring=n2a)
 
-        @pl.loop(0, n3a)
+        @pl.loop(0, n3a, unroll=4)
         def _(k):
             rem = [0.0, 0.0]
             for j in range(2):
@@ -326,7 +326,7 @@
                 B3[h, k, 8:8 + x3] = C3[h, k, 8:8 + x3] * (0.25 * (t + partner(t, 4)))
         w3 = level3()
 
-        @pl.loop(0, n3a)
+        @pl.loop(0, n3a, unroll=4)
         def _(k):
             for h in range(2):
                 v = w3[h, k, 8:8 + x3]
@@ -408,7 +408,7 @@
             sweep(WB, WA, BB, CC, 2, n0 - 2, 8, PXR, 1)
         solid = KEEP ** (2 if cyc == 0 else 6)
 
-        @pl.loop(0, own // 2)
+        @pl.loop(0, own // 2, unroll=2)
         def _(k):
             ra = remainder0(WB, H + 2 * k, solid)
             rb = remainder0(WB, H + 2 * k + 1, solid)

time: 106 us -> 102 us (0.962)
  Pallas kernels: 101 us -> 97.3 us
    pallas_call x1, Pallas kernels: 101 us -> 97.3 us  [per_device(): pl.pallas_call(functools.partial(kernel, ng, nz, A, X), out_shape=[jax.Sh...]
where the time goes in v2:
time: 102 us
  Pallas kernels  97.3 us (95%)
  local copies, waits for them, and re-layouts  3.39 us (3%)
    pallas_call x1, Pallas kernels, per_device(): pl.pallas_call(functools.partial(kernel, ng, nz, A, X), out_shape=[jax.Sh...  97.3 us
    unnamed x4, local copies, waits for them, and re-layouts  2.49 us

profile of v2, /device:TPU:0, one launch (start us, length us, event | category | flops | bytes accessed | tf_op | source)
XLA Modules:
  0.0 102.1 jit_solution(6700003421414309511)
XLA Ops:
  0.6 0.7 convert_element_type.3
  1.4 0.1 copy.9
  1.5 0.1 broadcast_in_dim.7
  1.5 0.7 copy.10.m_in
  2.3 97.3 %shard_map.50 = (f32[16,40,128]{2,1,0:T(8,128)}, f32[16,40,128]{2,1,0:T(8,128)}) custom-call(f32[16,40,128]{2,1,0:T(8,128)} %f_in.1, f32[16,40,128]{2,1,0:T(8,128)} %a_in.1, f32[4,40,128]{2,1,0:T(8,128)} %copy.10.m_in), custom_call_target="tpu_custom_call" | custom-call | tf_op jit(solution)/shard_map/pallas_call | solution.py:492
  99.6 0.0 copy-start
  99.6 1.8 %copy.13 = f32[16,40,128]{2,1,0:T(8,128)} copy(f32[16,40,128]{2,1,0:T(8,128)} %get-tuple-element.4) | data formatting | bytes 655360
  101.3 0.0 copy-done
  101.3 0.7 copy.14
  (2 shorter events, 0.0 us)
Async XLA Ops:
  99.6 1.8 %copy-start = (f32[16,40,128]{2,1,0:T(8,128)S(1)}, f32[16,40,128]{2,1,0:T(8,128)}, u32[]{:S(2)}) copy-start(f32[16,40,128]{2,1,0:T(8,128)} %get-tuple-element.5) | copy-start | bytes 983044
